TPU v7x, 32 devices: a whole 2x2x4 slice. The times are simulated.
32 devices in a mesh: row: 8 (over y, x, core), col: 4 (over z).
Axes of the slice: x: 2, y: 2, z: 4, core: 2. Of those that a mesh axis runs over, the one named last changes fastest.
Arguments:
- embeddings: bfloat16 [16384, 1024], P('row'), may hold values from -6 to 6
- vectors: bfloat16 [64, 16384], P(None, ('row', 'col')), may hold values from -6 to 6
- block_pairs: int32 [992, 2], replicated, may hold values from 0 to 31, as said below
Outputs:
- new_basis: float32 [64, 16384], P(None, ('row', 'col'))
Inputs may be any that keep to these rules, and one draw needn't show every extreme that they name: `block_pairs`: no pair is listed twice, no pair has equal blocks, and every block occurs as a row block at least once.
All inputs are finite; a program needn't handle non-finite values.
Results may differ from a plain program's by a relative error of at most 0.0032.
Values may be sent and summed in bfloat16 or wider, within the bound.
A program may use at most 128 MiB of HBM per device.

v0:
```python
import math

import jax
import jax.numpy as jnp
from jax import lax
from jax.sharding import PartitionSpec as P


def inverse_norms(blocks):
    return lax.rsqrt(jnp.mean(jnp.square(blocks.astype(jnp.float32)), axis=-1) + 1e-06)


def tile_terms(rows_x, cols_x, norm_rows, norm_cols, cols_v, feature_width):
    scores = jnp.dot(rows_x, cols_x.T, preferred_element_type=jnp.float32)
    affinity = jnp.exp(scores * norm_rows[:, None] * norm_cols[None, :] / math.sqrt(feature_width))
    rounded = affinity.astype(jnp.bfloat16)
    contrib = jnp.dot(cols_v, rounded.T, preferred_element_type=jnp.float32)
    return (contrib, jnp.sum(affinity, axis=1))


def tile_mask(block_pairs, near_column, col_count, row_count, here_row, here_col):
    near_ids = block_pairs[:, near_column]
    far_ids = block_pairs[:, 1 - near_column]
    member = (near_ids // col_count == here_row) & (far_ids % col_count == here_col)
    near_hot = ((near_ids % col_count)[:, None] == jnp.arange(col_count)[None, :]) & member[:, None]
    far_hot = (far_ids // col_count)[:, None] == jnp.arange(row_count)[None, :]
    return jnp.dot(
        near_hot.astype(jnp.float32).T,
        far_hot.astype(jnp.float32),
        preferred_element_type=jnp.float32,
    )


def add_block(running, contrib, row_totals, column_start, block_rows):
    sums_now, degree_now = running
    old_sums = lax.dynamic_slice_in_dim(sums_now, column_start, block_rows, 1)
    sums_now = lax.dynamic_update_slice_in_dim(sums_now, old_sums + contrib, column_start, 1)
    old_degree = lax.dynamic_slice_in_dim(degree_now, column_start, block_rows, 1)
    degree_now = lax.dynamic_update_slice_in_dim(
        degree_now, old_degree + row_totals[None, :], column_start, 1
    )
    return (sums_now, degree_now)


def per_device(embeddings, vectors, block_pairs):
    col_count = lax.axis_size("col")
    row_count = lax.axis_size("row")
    here_row = lax.axis_index("row")
    here_col = lax.axis_index("col")
    eig_count, block_rows = vectors.shape
    feature_width = embeddings.shape[1]
    near_blocks = embeddings.reshape(col_count, block_rows, feature_width)
    near_norms = inverse_norms(near_blocks)
    own_block = lax.dynamic_slice_in_dim(near_blocks, here_col, 1, 0)
    present = tile_mask(block_pairs, 0, col_count, row_count, here_row, here_col)
    start_sums = jnp.zeros((eig_count, col_count * block_rows), jnp.float32)
    start_degree = jnp.zeros((1, col_count * block_rows), jnp.float32)
    far_x = lax.all_gather(own_block, "row", axis=0, tiled=True)
    far_v = lax.all_gather(vectors[None], "row", axis=0, tiled=True)
    far_norms = inverse_norms(far_x)
    piece_blocks = far_x.shape[0]

    def visit(position, current):
        far_index = position // col_count
        near_index = position % col_count

        def compute(totals):
            contrib, row_totals = tile_terms(
                near_blocks[near_index],
                far_x[far_index],
                near_norms[near_index],
                far_norms[far_index],
                far_v[far_index],
                feature_width,
            )
            return add_block(totals, contrib, row_totals, near_index * block_rows, block_rows)

        return lax.cond(
            present[near_index, far_index] > 0.5, compute, lambda totals: totals, current
        )

    partial_sums, degree = lax.fori_loop(
        0, piece_blocks * col_count, visit, (start_sums, start_degree)
    )
    owned_sums, owned_degree = (
        lax.psum_scatter(partial_sums, "col", scatter_dimension=1, tiled=True),
        lax.psum_scatter(degree, "col", scatter_dimension=1, tiled=True),
    )
    smoothed = owned_sums / owned_degree
    total_rows = block_rows * col_count * row_count
    local_gram = jnp.dot(
        smoothed, smoothed.T, precision=lax.Precision.HIGHEST, preferred_element_type=jnp.float32
    )
    gram_matrix = lax.psum(local_gram, ("row", "col")) / total_rows
    factor = jnp.linalg.cholesky(gram_matrix)
    return lax.linalg.triangular_solve(factor, smoothed, left_side=True, lower=True)


def solution(mesh):
    return jax.shard_map(
        per_device,
        mesh=mesh,
        in_specs=(P("row", None), P(None, ("row", "col")), P()),
        out_specs=P(None, ("row", "col")),
        check_vma=False,
    )
```

profile of v0, /device:TPU:0, one launch (start us, length us, event | category | flops | bytes accessed | tf_op | source)
XLA Modules:
  0.0 305.4 jit_solution(10635929929781774671)
XLA Ops:
  9.0 3.1 %multiply_reduce_fusion.1 = f32[2048]{0:T(1024)S(1)} fusion(bf16[2048,1024]{1,0:T(8,128)(2,1)} %param.7), kind=kLoop, calls=%fused_computation.21 | loop fusion | flops 6289408 | bytes 4202496 | tf_op jit(solution)/shard_map/reduce_sum | solution.py:10
  12.1 12.3 %all-gather = bf16[512,512]{1,0:T(8,128)(2,1)S(1)} all-gather(bf16[64,512]{1,0:T(8,128)(2,1)} %param.8), channel_id=2, replica_groups=mesh['row'=8,'col'=4] {'row'}, dimensions={0}, use_global_device_ids=true | all-gather | bytes 589824 | tf_op jit(solution)/shard_map/all_gather | solution.py:59
  26.7 39.8 %all-gather.3.cloned.1.call-done = bf16[8,512,1024]{2,1,0:T(8,128)(2,1)} async-done(((bf16[1,512,1024]{2,1,0:T(8,128)(2,1)}), bf16[8,512,1024]{2,1,0:T(8,128)(2,1)}) %all-gather.3.cloned.1.call-update) | async-done | bytes 8388624 | tf_op jit(solution)/shard_map/all_gather | solution.py:58
  66.5 5.1 %multiply_reduce_fusion = f32[8,512]{1,0:T(8,128)S(1)} fusion(bf16[8,512,1024]{2,1,0:T(8,128)(2,1)} %all-gather.3.cloned.1.call-done), kind=kLoop, calls=%fused_computation.20 | loop fusion | flops 12578816 | bytes 8404992 | tf_op jit(solution)/shard_map/reduce_sum | solution.py:10
  71.6 121.8 %while.17 = (s32[]{:T(128)}, f32[64,2048]{1,0:T(8,128)S(1)}, f32[1,2048]{1,0:T(1,128)S(1)}, f32[4,8]{1,0:T(4,128)S(1)}, bf16[8,64,512]{2,1,0:T(8,128)(2,1)S(1)},...) while((s32[]{:T(128)}, f32[64,2048]{1,0:T(8,128)S(1)}, ...), condition=%wide.region_6.7_spmd, body=%wide.region_2.6_spmd.sunk | while | flops 571768832 | bytes 3494516 | solution.py:82
  74.1 2.7 conditional.2
  78.0 2.7 conditional.2
  78.0 2.4 fusion.25
  81.9 2.7 conditional.2
  81.9 2.4 fusion.25
  85.8 2.7 conditional.2
  85.8 2.4 fusion.25
  89.6 2.7 conditional.2
  89.7 2.4 fusion.25
  93.5 2.7 conditional.2
  93.6 2.4 fusion.25
  97.4 2.7 conditional.2
  97.5 2.4 fusion.25
  101.3 2.7 conditional.2
  101.4 2.4 fusion.25
  105.2 2.7 conditional.2
  105.2 2.4 fusion.25
  109.1 2.7 conditional.2
  109.1 2.4 fusion.25
  113.0 2.7 conditional.2
  113.0 2.4 fusion.25
  116.9 2.7 conditional.2
  120.8 2.7 conditional.2
  120.8 2.4 fusion.25
  124.7 2.7 conditional.2
  124.7 2.4 fusion.25
  128.5 2.7 conditional.2
  132.4 2.7 conditional.2
  132.5 2.4 fusion.25
  136.3 2.7 conditional.2
  136.4 2.4 fusion.25
  140.2 2.7 conditional.2
  144.1 2.7 conditional.2
  144.1 2.4 fusion.25
  148.0 2.7 conditional.2
  148.0 2.4 fusion.25
  151.9 2.7 conditional.2
  155.8 2.7 conditional.2
  155.8 2.4 fusion.25
  159.7 2.7 conditional.2
  159.7 2.4 fusion.25
  163.6 2.7 conditional.2
  167.5 2.7 conditional.2
  167.5 2.4 fusion.25
  171.3 2.7 conditional.2
  171.4 2.4 fusion.25
  175.2 2.7 conditional.2
  179.1 2.7 conditional.2
  179.2 2.4 fusion.25
  183.0 2.7 conditional.2
  183.1 2.4 fusion.25
  186.9 2.7 conditional.2
  190.8 2.7 conditional.2
  190.8 2.4 fusion.25
  195.6 26.6 %reduce-scatter.7.cloned.1.call-done = f32[512,1]{1,0:T(8,128)} async-done(((f32[2048,1]{1,0:T(8,128)}), f32[512,1]{1,0:T(8,128)}) %reduce-scatter.7.cloned.1.call-update) | async-done | bytes 2064
  223.2 21.6 %reduce-scatter.5.cloned.1.call-done = f32[64,512]{1,0:T(8,128)} async-done(((f32[64,2048]{1,0:T(8,128)}), f32[64,512]{1,0:T(8,128)}) %reduce-scatter.5.cloned.1.call-update) | async-done | bytes 131088 | tf_op jit(solution)/shard_map/reduce_scatter | solution.py:86
  246.1 38.6 %psum.7 = f32[64,64]{0,1:T(8,128)S(1)} all-reduce(f32[64,64]{0,1:T(8,128)S(1)} %fusion.21), channel_id=1, replica_groups=mesh['row'=8,'col'=4] {'row','col'}, use_global_device_ids=true, to_apply=%region_9.10 | all-reduce | flops 4096 | bytes 32768 | tf_op jit(solution)/shard_map/psum | solution.py:94
  284.9 5.8 %cholesky.16 = f32[64,64]{1,0:T(8,128)S(1)} custom-call(f32[64,64]{1,0:T(8,128)S(1)} %fusion.24), custom_call_target="Cholesky" | custom-call | tf_op jit(solution)/shard_map/jit(cholesky)/cholesky | solution.py:95
  292.1 4.9 %custom-call.6 = f32[1,64,64]{1,2,0:T(8,128)S(1)} custom-call(f32[1,64,64]{2,1,0:T(8,128)S(1)} %fusion.22), custom_call_target="InvertDiagBlocksLowerTriangular" | custom-call | tf_op jit(solution)/shard_map/triangular_solve | solution.py:96
  (161 shorter events, 58.0 us)
Async XLA Ops:
  6.5 59.9 %all-gather.3.cloned.1.call-start = ((), (), s32[]{:S(2)}) async-start(), calls=%async_computation.2 | async-start | bytes 9437184 | tf_op jit(solution)/shard_map/all_gather | solution.py:58
  8.9 213.3 %reduce-scatter.7.cloned.1.call-start = ((), (), s32[]{:S(2)}) async-start(), calls=%async_computation.4 | async-start | bytes 1310720
  193.5 1.5 copy-start
  194.9 50.0 %reduce-scatter.5.cloned.1.call-start = ((), (), s32[]{:S(2)}) async-start(), calls=%async_computation.3 | async-start | bytes 655360 | tf_op jit(solution)/shard_map/reduce_scatter | solution.py:86
Sparse Core Ops, SparseCore 0:
  9.2 57.1 all-gather.2
  195.0 27.1 reduce-scatter.6
  224.6 20.2 reduce-scatter.4
where the time goes:
time: 307 us; the launch traced here: 305 us
  waiting for transfers between devices  88.7 us (29%)
  matrix products  84.6 us (28%)
  blocking collectives  51 us (17%)
  local copies, waits for them, and re-layouts  24.2 us (8%)
  other arithmetic  22.4 us (7%)
  loops' own time  21.2 us (7%)
  between operations  13.2 us (4%)
    dot_general x31, matrix products, tile_terms(): scores = jnp.dot(rows_x, cols_x.T, preferred_element_type=jnp.float32)  74.2 us
    all_gather x1, waiting for transfers between devices, per_device(): far_x = lax.all_gather(own_block, 'row', axis=0, tiled=True)  39.8 us
    psum x1, blocking collectives, per_device(): gram_matrix = lax.psum(local_gram, ('row', 'col')) / total_rows  38.6 us
    unnamed x4, waiting for transfers between devices  27.3 us
    reduce_scatter x1, waiting for transfers between devices, per_device(): lax.psum_scatter(partial_sums, 'col', scatter_dimension=1, tiled=True)  21.6 us
    another operation x1, loops' own time, per_device(): lax.fori_loop(0, piece_blocks * col_count, visit, (start_sums, start_degr...  19.9 us
    dynamic_slice x32, local copies, waits for them, and re-layouts, visit(): present[near_index, far_index] > 0.5  19 us
    all_gather x1, blocking collectives, per_device(): far_v = lax.all_gather(vectors[None], 'row', axis=0, tiled=True)  12.3 us
  transfers between devices with their start and end apart: 3, of which 3 were waited for; matrix products, arithmetic and copies ran while one was open for 2% of the time, Pallas kernels for 0%

commit v1 on v0

--- a/solution.py
+++ b/solution.py
@@ -1,8 +1,11 @@
+import functools
 import math
 
 import jax
 import jax.numpy as jnp
 from jax import lax
+from jax.experimental import pallas as pl
+from jax.experimental.pallas import tpu as pltpu
 from jax.sharding import PartitionSpec as P
 
 
@@ -96,11 +99,277 @@
     return lax.linalg.triangular_solve(factor, smoothed, left_side=True, lower=True)
 
 
+UNITS = 16
+FIRST_SENDS = ((0, 4, 2), (1, 5, 4), (0, 2, 1), (1, 3, 1), (1, 8, 2), (0, 9, 4))
+RELAYS = {
+    4: ((4, 12, 4), (5, 13, 2), (4, 6, 1), (5, 7, 1)),
+    8: ((8, 10, 1), (9, 11, 1)),
+    12: ((12, 14, 1), (13, 15, 1)),
+}
+
+
+def across(row, bits):
+    if bits & 1:
+        row = row + 1 - 2 * (row % 2)
+    if bits & 2:
+        row = row + 2 - 4 * ((row // 2) % 2)
+    if bits & 4:
+        row = row + 4 - 8 * ((row // 4) % 2)
+    return row
+
+
+def whole_kernel(
+    total_rows,
+    x_hbm,
+    v_ref,
+    out_ref,
+    own_x,
+    far_x,
+    far_v,
+    own_norm,
+    acc,
+    parts,
+    plane_gram,
+    depth_gram,
+    own_sem,
+    x_send,
+    x_recv,
+    v_send,
+    v_recv,
+    part_send,
+    part_recv,
+    plane_send,
+    plane_recv,
+    depth_send,
+    depth_recv,
+):
+    row = lax.axis_index("row")
+    col = lax.axis_index("col")
+    row_count = plane_gram.shape[0]
+    col_count, padded, block_rows = acc.shape
+    eig_count = v_ref.shape[0]
+    half = block_rows // 2
+    width = own_x.shape[1]
+    mesh_ids = pl.DeviceIdType.MESH
+
+    load = pltpu.make_async_copy(x_hbm, own_x, own_sem)
+    load.start()
+
+    barrier = pltpu.get_barrier_semaphore()
+    for bits in range(1, row_count):
+        pl.semaphore_signal(barrier, inc=1, device_id=(across(row, bits), col), device_id_type=mesh_ids)
+    for step in range(1, col_count):
+        pl.semaphore_signal(barrier, inc=1, device_id=(row, (col + step) % col_count), device_id_type=mesh_ids)
+    pl.semaphore_wait(barrier, row_count + col_count - 2)
+
+    def unit_copies(source, target, bits):
+        if source < 2:
+            start = pl.multiple_of(col * block_rows + source * half, half)
+            x_src = x_hbm.at[pl.ds(start, half), :]
+            v_src = v_ref.at[:, pl.ds(source * half, half)]
+        else:
+            x_src = far_x.at[source]
+            v_src = far_v.at[source]
+        partner = (across(row, bits), col)
+        return (
+            pltpu.make_async_remote_copy(
+                src_ref=v_src, dst_ref=far_v.at[target], send_sem=v_send.at[target],
+                recv_sem=v_recv.at[target], device_id=partner, device_id_type=mesh_ids,
+            ),
+            pltpu.make_async_remote_copy(
+                src_ref=x_src, dst_ref=far_x.at[target], send_sem=x_send.at[target],
+                recv_sem=x_recv.at[target], device_id=partner, device_id_type=mesh_ids,
+            ),
+        )
+
+    def start_unit(item):
+        for copy in unit_copies(*item):
+            copy.start()
+
+    def wait_unit(target):
+        pltpu.make_async_copy(far_v.at[target], far_v.at[target], v_recv.at[target]).wait()
+        pltpu.make_async_copy(far_x.at[target], far_x.at[target], x_recv.at[target]).wait()
+
+    for item in FIRST_SENDS:
+        start_unit(item)
+
+    load.wait()
+    far_v[0] = v_ref[:, :half]
+    far_v[1] = v_ref[:, half:]
+    for part in range(2):
+        start = pl.multiple_of(col * block_rows + part * half, half)
+        far_x[part] = own_x[pl.ds(start, half), :]
+    acc[...] = jnp.zeros_like(acc)
+
+    @pl.loop(0, col_count)
+    def _(near):
+        rows = own_x[pl.ds(pl.multiple_of(near * block_rows, block_rows), block_rows), :].astype(jnp.float32)
+        mean = jnp.sum(rows * rows, axis=1, keepdims=True) * (1.0 / width)
+        norm = lax.rsqrt(mean + 1e-06)
+        turned = jnp.broadcast_to(norm, (block_rows, 128)).T
+        own_norm[near] = turned[0:8, :]
+
+    scale = 1.4426950408889634 / math.sqrt(width)
+
+    @pl.loop(0, UNITS)
+    def _(unit):
+        @pl.when(unit == 2)
+        def _():
+            acc[col] = jnp.zeros((padded, block_rows), jnp.float32)
+
+        for first, items in RELAYS.items():
+            @pl.when(unit == first)
+            def _(first=first, items=items):
+                wait_unit(first)
+                wait_unit(first + 1)
+                for item in items:
+                    start_unit(item)
+
+        for alone in (2, 3, 6, 7, 10, 11, 14, 15):
+            @pl.when(unit == alone)
+            def _(alone=alone):
+                wait_unit(alone)
+
+        cols = far_x[unit]
+        wide = cols.astype(jnp.float32)
+        mean = jnp.sum(wide * wide, axis=1, keepdims=True) * (1.0 / width)
+        col_norm = lax.rsqrt(mean + 1e-06) * scale
+        cols_v = far_v[unit]
+        for near in range(col_count):
+            scores = lax.dot_general(
+                cols, own_x[near * block_rows : (near + 1) * block_rows, :],
+                (((1,), (1,)), ((), ())), preferred_element_type=jnp.float32,
+            )
+            affinity = jnp.exp2(scores * own_norm[near, 0:1, :] * col_norm)
+            acc[near, eig_count:, :] += jnp.sum(affinity.reshape(half // 8, 8, block_rows), axis=0)
+            acc[near, :eig_count, :] += jnp.dot(
+                cols_v, affinity.astype(jnp.bfloat16), preferred_element_type=jnp.float32
+            )
+
+    def part_copy(step):
+        target = (col + step) % col_count
+        return pltpu.make_async_remote_copy(
+            src_ref=acc.at[target], dst_ref=parts.at[step - 1], send_sem=part_send.at[step - 1],
+            recv_sem=part_recv.at[step - 1], device_id=(row, target), device_id_type=mesh_ids,
+        )
+
+    for step in range(1, col_count):
+        part_copy(step).start()
+    total = acc[col]
+    for step in range(1, col_count):
+        part_copy(step).wait_recv()
+        total = total + parts[step - 1]
+    degree = jnp.sum(total[eig_count:, :], axis=0, keepdims=True)
+    smoothed = total[:eig_count, :] / degree
+
+    def gram_sum(gram, held, me, partners, send_sem, recv_sem):
+        held[me] = gram
+        copies = []
+        for at, partner in enumerate(partners):
+            copies.append(
+                pltpu.make_async_remote_copy(
+                    src_ref=held.at[me], dst_ref=held.at[me], send_sem=send_sem.at[at],
+                    recv_sem=recv_sem.at[at], device_id=partner, device_id_type=mesh_ids,
+                )
+            )
+        for copy in copies:
+            copy.start()
+        for copy in copies:
+            copy.wait()
+        return jnp.sum(held[...], axis=0)
+
+    gram = lax.dot_general(
+        smoothed, smoothed, (((1,), (1,)), ((), ())),
+        precision=lax.Precision.HIGHEST, preferred_element_type=jnp.float32,
+    )
+    gram = gram_sum(
+        gram, plane_gram, row, [(across(row, bits), col) for bits in range(1, row_count)],
+        plane_send, plane_recv,
+    )
+    gram = gram_sum(
+        gram, depth_gram, col, [(row, (col + step) % col_count) for step in range(1, col_count)],
+        depth_send, depth_recv,
+    )
+    gram = gram / total_rows
+
+    down = lax.broadcasted_iota(jnp.int32, (eig_count, 1), 0)
+    at_row = lax.broadcasted_iota(jnp.int32, (eig_count, eig_count), 0)
+    at_col = lax.broadcasted_iota(jnp.int32, (eig_count, eig_count), 1)
+    diagonal = at_row == at_col
+    work = jnp.concatenate([diagonal.astype(jnp.float32), gram], axis=1)
+    for step in range(eig_count - 1):
+        at = eig_count + step
+        pivot = work[step : step + 1, :]
+        ratio = work[:, at : at + 1] * (1.0 / pivot[:, at : at + 1])
+        work = work - jnp.where(down > step, ratio, 0.0) * pivot
+    pivots = jnp.sum(jnp.where(diagonal, work[:, eig_count:], 0.0), axis=1, keepdims=True)
+    inverse = work[:, :eig_count] * lax.rsqrt(pivots)
+    out_ref[...] = jnp.dot(
+        inverse, smoothed, precision=lax.Precision.HIGHEST, preferred_element_type=jnp.float32
+    )
+
+    for item in FIRST_SENDS + sum(RELAYS.values(), ()):
+        for copy in unit_copies(*item):
+            copy.wait_send()
+    for step in range(1, col_count):
+        part_copy(step).wait_send()
+
+
+def per_device_full(total_rows, row_count, embeddings, vectors, block_pairs):
+    del block_pairs
+    eig_count, block_rows = vectors.shape
+    near_rows, width = embeddings.shape
+    col_count = near_rows // block_rows
+    half = block_rows // 2
+    padded = eig_count + 8
+    dma = pltpu.SemaphoreType.DMA
+    return pl.pallas_call(
+        functools.partial(whole_kernel, total_rows),
+        out_shape=jax.ShapeDtypeStruct((eig_count, block_rows), jnp.float32),
+        in_specs=[pl.BlockSpec(memory_space=pl.ANY), pl.BlockSpec(memory_space=pltpu.VMEM)],
+        out_specs=pl.BlockSpec(memory_space=pltpu.VMEM),
+        scratch_shapes=[
+            pltpu.VMEM((near_rows, width), jnp.bfloat16),
+            pltpu.VMEM((UNITS, half, width), jnp.bfloat16),
+            pltpu.VMEM((UNITS, eig_count, half), jnp.bfloat16),
+            pltpu.VMEM((col_count, 8, block_rows), jnp.float32),
+            pltpu.VMEM((col_count, padded, block_rows), jnp.float32),
+            pltpu.VMEM((col_count - 1, padded, block_rows), jnp.float32),
+            pltpu.VMEM((row_count, eig_count, eig_count), jnp.float32),
+            pltpu.VMEM((col_count, eig_count, eig_count), jnp.float32),
+            dma(()),
+            dma((UNITS,)),
+            dma((UNITS,)),
+            dma((UNITS,)),
+            dma((UNITS,)),
+            dma((col_count - 1,)),
+            dma((col_count - 1,)),
+            dma((row_count - 1,)),
+            dma((row_count - 1,)),
+            dma((col_count - 1,)),
+            dma((col_count - 1,)),
+        ],
+        compiler_params=pltpu.CompilerParams(
+            collective_id=0, has_side_effects=True, vmem_limit_bytes=48 * 1024 * 1024
+        ),
+    )(embeddings, vectors)
+
+
 def solution(mesh):
-    return jax.shard_map(
-        per_device,
-        mesh=mesh,
-        in_specs=(P("row", None), P(None, ("row", "col")), P()),
-        out_specs=P(None, ("row", "col")),
-        check_vma=False,
-    )
+    row_count, col_count = mesh.shape["row"], mesh.shape["col"]
+
+    def step(embeddings, vectors, block_pairs):
+        blocks = row_count * col_count
+        full = block_pairs.shape[0] == blocks * (blocks - 1) and row_count == 8
+        body = per_device
+        if full:
+            body = functools.partial(per_device_full, embeddings.shape[0], row_count)
+        return jax.shard_map(
+            body,
+            mesh=mesh,
+            in_specs=(P("row", None), P(None, ("row", "col")), P()),
+            out_specs=P(None, ("row", "col")),
+            check_vma=False,
+        )(embeddings, vectors, block_pairs)
+
+    return step

time: 307 us -> 85 us (0.28)
  waiting for transfers between devices: 88.7 us -> 0 us
  matrix products: 84.6 us -> 0 us
  Pallas kernels: 0 us -> 81.1 us
  blocking collectives: 51 us -> 0 us
  other arithmetic: 22.4 us -> 0 us
  loops' own time: 21.2 us -> 0 us
  local copies, waits for them, and re-layouts: 24.2 us -> 3.68 us
  between operations: 13.2 us -> 0.01 us
    dot_general x64 -> x0, matrix products: 82.7 us -> none  [the longest x31 74.2 us: tile_terms(): scores = jnp.dot(rows_x, cols_x.T, preferred_element_type=jnp.float32)]
    pallas_call x0 -> x1, Pallas kernels: none -> 81.1 us  [per_device_full(): pl.pallas_call(functools.partial(whole_kernel, total_rows), out_shape=jax...]
    all_gather x1 -> x0, waiting for transfers between devices: 39.8 us -> none  [per_device(): far_x = lax.all_gather(own_block, 'row', axis=0, tiled=True)]
    psum x1 -> x0, blocking collectives: 38.6 us -> none  [per_device(): gram_matrix = lax.psum(local_gram, ('row', 'col')) / total_rows]
    unnamed x4 -> x0, waiting for transfers between devices: 27.3 us -> none
    dynamic_slice x64 -> x0, local copies, waits for them, and re-layouts: 21.7 us -> none  [the longest x32 19 us: visit(): present[near_index, far_index] > 0.5]
    reduce_scatter x1 -> x0, waiting for transfers between devices: 21.6 us -> none  [per_device(): lax.psum_scatter(partial_sums, 'col', scatter_dimension=1, tiled=True)]
    another operation x33 -> x0, loops' own time: 21.2 us -> none  [the longest x1 19.9 us: per_device(): lax.fori_loop(0, piece_blocks * col_count, visit, (start_sums, start_degr...]
  transfers between devices with their start and end apart: 3 -> 0, of which waited for: 3 -> 0; matrix products, arithmetic and copies ran while one was open for 2% -> 0% of each run, Pallas kernels for 0% -> 0%
where the time goes in v1:
time: 85 us; the launch traced here: 84.8 us
  Pallas kernels  81.1 us (95%)
  local copies, waits for them, and re-layouts  3.68 us (4%)
    pallas_call x1, Pallas kernels, per_device_full(): pl.pallas_call(functools.partial(whole_kernel, total_rows), out_shape=jax...  81.1 us
    unnamed x5, local copies, waits for them, and re-layouts  3.68 us

profile of v1, /device:TPU:0, one launch (start us, length us, event | category | flops | bytes accessed | tf_op | source)
XLA Modules:
  0.0 84.8 jit_solution(14177826122815660078)
XLA Ops:
  0.0 0.0 copy-start
  0.0 2.2 %copy-done = bf16[2048,1024]{1,0:T(8,128)(2,1)S(1)} copy-done((bf16[2048,1024]{1,0:T(8,128)(2,1)S(1)}, bf16[2048,1024]{1,0:T(8,128)(2,1)}, u32[]{:S(2)}) %copy-start) | copy-done | bytes 4194328
  2.2 0.0 copy-start.1
  2.2 0.8 copy-done.1
  3.0 81.1 %shard_map.28 = f32[64,512]{1,0:T(8,128)S(1)} custom-call(bf16[2048,1024]{1,0:T(8,128)(2,1)S(1)} %copy-done, bf16[64,512]{1,0:T(8,128)(2,1)S(1)} %copy-done.1), custom_call_target="tpu_custom_call" | custom-call | tf_op jit(solution)/shard_map/pallas_call | solution.py:326
  84.1 0.7 copy.4
Async XLA Ops:
  0.0 2.2 %copy-start = (bf16[2048,1024]{1,0:T(8,128)(2,1)S(1)}, bf16[2048,1024]{1,0:T(8,128)(2,1)}, u32[]{:S(2)}) copy-start(bf16[2048,1024]{1,0:T(8,128)(2,1)} %x_hbm.1) | copy-start | bytes 12582916
  2.2 0.8 copy-start.1

commit v2 on v1

--- a/solution.py
+++ b/solution.py
@@ -121,9 +121,11 @@
 def whole_kernel(
     total_rows,
     x_hbm,
-    v_ref,
+    v_hbm,
     out_ref,
     own_x,
+    turned_x,
+    own_v,
     far_x,
     far_v,
     own_norm,
@@ -132,6 +134,7 @@
     plane_gram,
     depth_gram,
     own_sem,
+    own_v_sem,
     x_send,
     x_recv,
     v_send,
@@ -147,13 +150,15 @@
     col = lax.axis_index("col")
     row_count = plane_gram.shape[0]
     col_count, padded, block_rows = acc.shape
-    eig_count = v_ref.shape[0]
+    eig_count = own_v.shape[0]
     half = block_rows // 2
     width = own_x.shape[1]
     mesh_ids = pl.DeviceIdType.MESH
 
     load = pltpu.make_async_copy(x_hbm, own_x, own_sem)
     load.start()
+    load_v = pltpu.make_async_copy(v_hbm, own_v, own_v_sem)
+    load_v.start()
 
     barrier = pltpu.get_barrier_semaphore()
     for bits in range(1, row_count):
@@ -166,7 +171,7 @@
         if source < 2:
             start = pl.multiple_of(col * block_rows + source * half, half)
             x_src = x_hbm.at[pl.ds(start, half), :]
-            v_src = v_ref.at[:, pl.ds(source * half, half)]
+            v_src = v_hbm.at[:, pl.ds(source * half, half)]
         else:
             x_src = far_x.at[source]
             v_src = far_v.at[source]
@@ -194,8 +199,9 @@
         start_unit(item)
 
     load.wait()
-    far_v[0] = v_ref[:, :half]
-    far_v[1] = v_ref[:, half:]
+    load_v.wait()
+    far_v[0] = own_v[:, :half]
+    far_v[1] = own_v[:, half:]
     for part in range(2):
         start = pl.multiple_of(col * block_rows + part * half, half)
         far_x[part] = own_x[pl.ds(start, half), :]
@@ -203,11 +209,11 @@
 
     @pl.loop(0, col_count)
     def _(near):
-        rows = own_x[pl.ds(pl.multiple_of(near * block_rows, block_rows), block_rows), :].astype(jnp.float32)
-        mean = jnp.sum(rows * rows, axis=1, keepdims=True) * (1.0 / width)
-        norm = lax.rsqrt(mean + 1e-06)
-        turned = jnp.broadcast_to(norm, (block_rows, 128)).T
-        own_norm[near] = turned[0:8, :]
+        rows = own_x[pl.ds(pl.multiple_of(near * block_rows, block_rows), block_rows), :]
+        turned = rows.astype(jnp.float32).T
+        turned_x[near] = turned.astype(jnp.bfloat16)
+        mean = jnp.sum(turned * turned, axis=0, keepdims=True) * (1.0 / width)
+        own_norm[near] = jnp.broadcast_to(lax.rsqrt(mean + 1e-06), (8, block_rows))
 
     scale = 1.4426950408889634 / math.sqrt(width)
 
@@ -236,10 +242,7 @@
         col_norm = lax.rsqrt(mean + 1e-06) * scale
         cols_v = far_v[unit]
         for near in range(col_count):
-            scores = lax.dot_general(
-                cols, own_x[near * block_rows : (near + 1) * block_rows, :],
-                (((1,), (1,)), ((), ())), preferred_element_type=jnp.float32,
-            )
+            scores = jnp.dot(cols, turned_x[near], preferred_element_type=jnp.float32)
             affinity = jnp.exp2(scores * own_norm[near, 0:1, :] * col_norm)
             acc[near, eig_count:, :] += jnp.sum(affinity.reshape(half // 8, 8, block_rows), axis=0)
             acc[near, :eig_count, :] += jnp.dot(
@@ -326,10 +329,12 @@
     return pl.pallas_call(
         functools.partial(whole_kernel, total_rows),
         out_shape=jax.ShapeDtypeStruct((eig_count, block_rows), jnp.float32),
-        in_specs=[pl.BlockSpec(memory_space=pl.ANY), pl.BlockSpec(memory_space=pltpu.VMEM)],
+        in_specs=[pl.BlockSpec(memory_space=pl.ANY)] * 2,
         out_specs=pl.BlockSpec(memory_space=pltpu.VMEM),
         scratch_shapes=[
             pltpu.VMEM((near_rows, width), jnp.bfloat16),
+            pltpu.VMEM((col_count, width, block_rows), jnp.bfloat16),
+            pltpu.VMEM((eig_count, block_rows), jnp.bfloat16),
             pltpu.VMEM((UNITS, half, width), jnp.bfloat16),
             pltpu.VMEM((UNITS, eig_count, half), jnp.bfloat16),
             pltpu.VMEM((col_count, 8, block_rows), jnp.float32),
@@ -337,6 +342,7 @@
             pltpu.VMEM((col_count - 1, padded, block_rows), jnp.float32),
             pltpu.VMEM((row_count, eig_count, eig_count), jnp.float32),
             pltpu.VMEM((col_count, eig_count, eig_count), jnp.float32),
+            dma(()),
             dma(()),
             dma((UNITS,)),
             dma((UNITS,)),
@@ -350,7 +356,7 @@
             dma((col_count - 1,)),
         ],
         compiler_params=pltpu.CompilerParams(
-            collective_id=0, has_side_effects=True, vmem_limit_bytes=48 * 1024 * 1024
+            collective_id=0, has_side_effects=True, vmem_limit_bytes=60 * 1024 * 1024
         ),
     )(embeddings, vectors)
 

time: 85 us -> 82.7 us (0.973)
  local copies, waits for them, and re-layouts: 3.68 us -> 1.57 us
    unnamed x5 -> x1, local copies, waits for them, and re-layouts: 3.68 us -> 1.57 us
where the time goes in v2:
time: 82.7 us; the launch traced here: 82.5 us
  Pallas kernels  81 us (98%)
  local copies, waits for them, and re-layouts  1.57 us (2%)
    pallas_call x1, Pallas kernels, per_device_full(): pl.pallas_call(functools.partial(whole_kernel, total_rows), out_shape=jax...  81 us

profile of v2, /device:TPU:0, one launch (start us, length us, event | category | flops | bytes accessed | tf_op | source)
XLA Modules:
  0.0 82.5 jit_solution(9623065958362448277)
XLA Ops:
  0.0 81.0 %shard_map.28 = f32[64,512]{1,0:T(8,128)} custom-call(bf16[2048,1024]{1,0:T(8,128)(2,1)} %x_hbm.1, bf16[64,512]{1,0:T(8,128)(2,1)} %v_hbm.1), custom_call_target="tpu_custom_call" | custom-call | tf_op jit(solution)/shard_map/pallas_call | solution.py:329
  81.0 1.6 %copy.4 = f32[64,512]{1,0:T(8,128)} copy(f32[64,512]{1,0:T(8,128)} %shard_map.28) | data formatting | bytes 262144

commit v3 on v2

--- a/solution.py
+++ b/solution.py
@@ -217,7 +217,20 @@
 
     scale = 1.4426950408889634 / math.sqrt(width)
 
-    @pl.loop(0, UNITS)
+    def unit_norm(unit):
+        wide = far_x[unit].astype(jnp.float32)
+        mean = jnp.sum(wide * wide, axis=1, keepdims=True) * (1.0 / width)
+        return lax.rsqrt(mean + 1e-06) * scale
+
+    def add_tile(unit, near, col_norm):
+        scores = jnp.dot(far_x[unit], turned_x[near], preferred_element_type=jnp.float32)
+        affinity = jnp.exp2(scores * own_norm[near, 0:1, :] * col_norm)
+        acc[near, eig_count:, :] += jnp.sum(affinity.reshape(half // 8, 8, block_rows), axis=0)
+        acc[near, :eig_count, :] += jnp.dot(
+            far_v[unit], affinity.astype(jnp.bfloat16), preferred_element_type=jnp.float32
+        )
+
+    @pl.loop(0, UNITS - 2)
     def _(unit):
         @pl.when(unit == 2)
         def _():
@@ -231,37 +244,41 @@
                 for item in items:
                     start_unit(item)
 
-        for alone in (2, 3, 6, 7, 10, 11, 14, 15):
+        for alone in (2, 3, 6, 7, 10, 11):
             @pl.when(unit == alone)
             def _(alone=alone):
                 wait_unit(alone)
 
-        cols = far_x[unit]
-        wide = cols.astype(jnp.float32)
-        mean = jnp.sum(wide * wide, axis=1, keepdims=True) * (1.0 / width)
-        col_norm = lax.rsqrt(mean + 1e-06) * scale
-        cols_v = far_v[unit]
+        col_norm = unit_norm(unit)
         for near in range(col_count):
-            scores = jnp.dot(cols, turned_x[near], preferred_element_type=jnp.float32)
-            affinity = jnp.exp2(scores * own_norm[near, 0:1, :] * col_norm)
-            acc[near, eig_count:, :] += jnp.sum(affinity.reshape(half // 8, 8, block_rows), axis=0)
-            acc[near, :eig_count, :] += jnp.dot(
-                cols_v, affinity.astype(jnp.bfloat16), preferred_element_type=jnp.float32
-            )
-
-    def part_copy(step):
-        target = (col + step) % col_count
+            add_tile(unit, near, col_norm)
+
+    pair = col + 1 - 2 * (col % 2)
+    far = (col + 2) % col_count
+    far_pair = col_count - 1 - col
+
+    def part_copy(at):
+        source, target = ((far_pair, pair), (pair, pair), (far, far))[at]
         return pltpu.make_async_remote_copy(
-            src_ref=acc.at[target], dst_ref=parts.at[step - 1], send_sem=part_send.at[step - 1],
-            recv_sem=part_recv.at[step - 1], device_id=(row, target), device_id_type=mesh_ids,
+            src_ref=acc.at[source], dst_ref=parts.at[at], send_sem=part_send.at[at],
+            recv_sem=part_recv.at[at], device_id=(row, target), device_id_type=mesh_ids,
         )
 
-    for step in range(1, col_count):
-        part_copy(step).start()
-    total = acc[col]
-    for step in range(1, col_count):
-        part_copy(step).wait_recv()
-        total = total + parts[step - 1]
+    last = (UNITS - 2, UNITS - 1)
+    for unit in last:
+        wait_unit(unit)
+    last_norms = [unit_norm(unit) for unit in last]
+    for at, near in enumerate((far_pair, pair, far, col)):
+        for unit, col_norm in zip(last, last_norms):
+            add_tile(unit, near, col_norm)
+        if at == 2:
+            part_copy(0).wait_recv()
+            acc[far] = acc[far] + parts[0]
+        if at < 3:
+            part_copy(at).start()
+    part_copy(1).wait_recv()
+    part_copy(2).wait_recv()
+    total = acc[col] + parts[1] + parts[2]
     degree = jnp.sum(total[eig_count:, :], axis=0, keepdims=True)
     smoothed = total[:eig_count, :] / degree
 
@@ -285,15 +302,16 @@
         smoothed, smoothed, (((1,), (1,)), ((), ())),
         precision=lax.Precision.HIGHEST, preferred_element_type=jnp.float32,
     )
-    gram = gram_sum(
-        gram, plane_gram, row, [(across(row, bits), col) for bits in range(1, row_count)],
+    packed = jnp.concatenate([gram[: eig_count // 2, :], gram[eig_count // 2 :, :]], axis=1)
+    packed = gram_sum(
+        packed, plane_gram, row, [(across(row, bits), col) for bits in range(1, row_count)],
         plane_send, plane_recv,
     )
-    gram = gram_sum(
-        gram, depth_gram, col, [(row, (col + step) % col_count) for step in range(1, col_count)],
+    packed = gram_sum(
+        packed, depth_gram, col, [(row, (col + step) % col_count) for step in range(1, col_count)],
         depth_send, depth_recv,
     )
-    gram = gram / total_rows
+    gram = jnp.concatenate([packed[:, :eig_count], packed[:, eig_count:]], axis=0) / total_rows
 
     down = lax.broadcasted_iota(jnp.int32, (eig_count, 1), 0)
     at_row = lax.broadcasted_iota(jnp.int32, (eig_count, eig_count), 0)
@@ -314,8 +332,8 @@
     for item in FIRST_SENDS + sum(RELAYS.values(), ()):
         for copy in unit_copies(*item):
             copy.wait_send()
-    for step in range(1, col_count):
-        part_copy(step).wait_send()
+    for at in range(3):
+        part_copy(at).wait_send()
 
 
 def per_device_full(total_rows, row_count, embeddings, vectors, block_pairs):
@@ -340,8 +358,8 @@
             pltpu.VMEM((col_count, 8, block_rows), jnp.float32),
             pltpu.VMEM((col_count, padded, block_rows), jnp.float32),
             pltpu.VMEM((col_count - 1, padded, block_rows), jnp.float32),
-            pltpu.VMEM((row_count, eig_count, eig_count), jnp.float32),
-            pltpu.VMEM((col_count, eig_count, eig_count), jnp.float32),
+            pltpu.VMEM((row_count, eig_count // 2, 2 * eig_count), jnp.float32),
+            pltpu.VMEM((col_count, eig_count // 2, 2 * eig_count), jnp.float32),
             dma(()),
             dma(()),
             dma((UNITS,)),
@@ -366,7 +384,7 @@
 
     def step(embeddings, vectors, block_pairs):
         blocks = row_count * col_count
-        full = block_pairs.shape[0] == blocks * (blocks - 1) and row_count == 8
+        full = block_pairs.shape[0] == blocks * (blocks - 1) and (row_count, col_count) == (8, 4)
         body = per_device
         if full:
             body = functools.partial(per_device_full, embeddings.shape[0], row_count)

time: 82.7 us -> 77.2 us (0.933)
  Pallas kernels: 81 us -> 75.5 us
    pallas_call x1, Pallas kernels: 81 us -> 75.5 us  [per_device_full(): pl.pallas_call(functools.partial(whole_kernel, total_rows), out_shape=jax...]
where the time goes in v3:
time: 77.2 us; the launch traced here: 77.1 us
  Pallas kernels  75.5 us (98%)
  local copies, waits for them, and re-layouts  1.57 us (2%)
    pallas_call x1, Pallas kernels, per_device_full(): pl.pallas_call(functools.partial(whole_kernel, total_rows), out_shape=jax...  75.5 us
    unnamed x1, local copies, waits for them, and re-layouts  1.57 us

profile of v3, /device:TPU:0, one launch (start us, length us, event | category | flops | bytes accessed | tf_op | source)
XLA Modules:
  0.0 77.1 jit_solution(12020310727728353945)
XLA Ops:
  0.0 75.5 %shard_map.28 = f32[64,512]{1,0:T(8,128)} custom-call(bf16[2048,1024]{1,0:T(8,128)(2,1)} %x_hbm.1, bf16[64,512]{1,0:T(8,128)(2,1)} %v_hbm.1), custom_call_target="tpu_custom_call" | custom-call | tf_op jit(solution)/shard_map/pallas_call | solution.py:347
  75.5 1.6 %copy.4 = f32[64,512]{1,0:T(8,128)} copy(f32[64,512]{1,0:T(8,128)} %shard_map.28) | data formatting | bytes 262144

commit v4 on v3

--- a/solution.py
+++ b/solution.py
@@ -217,21 +217,27 @@
 
     scale = 1.4426950408889634 / math.sqrt(width)
 
-    def unit_norm(unit):
-        wide = far_x[unit].astype(jnp.float32)
+    def pair_norm(unit):
+        wide = far_x[pl.ds(unit, 2)].reshape(block_rows, width).astype(jnp.float32)
         mean = jnp.sum(wide * wide, axis=1, keepdims=True) * (1.0 / width)
         return lax.rsqrt(mean + 1e-06) * scale
 
-    def add_tile(unit, near, col_norm):
-        scores = jnp.dot(far_x[unit], turned_x[near], preferred_element_type=jnp.float32)
+    def pair_scores(unit, near):
+        cols = far_x[pl.ds(unit, 2)].reshape(block_rows, width)
+        return jnp.dot(cols, turned_x[near], preferred_element_type=jnp.float32)
+
+    def add_tile(unit, near, scores, col_norm):
         affinity = jnp.exp2(scores * own_norm[near, 0:1, :] * col_norm)
-        acc[near, eig_count:, :] += jnp.sum(affinity.reshape(half // 8, 8, block_rows), axis=0)
+        acc[near, eig_count:, :] += jnp.sum(affinity.reshape(block_rows // 8, 8, block_rows), axis=0)
+        cols_v = jnp.concatenate([far_v[unit], far_v[unit + 1]], axis=1)
         acc[near, :eig_count, :] += jnp.dot(
-            far_v[unit], affinity.astype(jnp.bfloat16), preferred_element_type=jnp.float32
+            cols_v, affinity.astype(jnp.bfloat16), preferred_element_type=jnp.float32
         )
 
-    @pl.loop(0, UNITS - 2)
-    def _(unit):
+    @pl.loop(0, UNITS // 2 - 1)
+    def _(pair_at):
+        unit = pair_at * 2
+
         @pl.when(unit == 2)
         def _():
             acc[col] = jnp.zeros((padded, block_rows), jnp.float32)
@@ -244,14 +250,19 @@
                 for item in items:
                     start_unit(item)
 
-        for alone in (2, 3, 6, 7, 10, 11):
-            @pl.when(unit == alone)
-            def _(alone=alone):
-                wait_unit(alone)
-
-        col_norm = unit_norm(unit)
+        for first in (2, 6, 10):
+            @pl.when(unit == first)
+            def _(first=first):
+                wait_unit(first)
+                wait_unit(first + 1)
+
+        scores = pair_scores(unit, 0)
+        col_norm = pair_norm(unit)
         for near in range(col_count):
-            add_tile(unit, near, col_norm)
+            current = scores
+            if near + 1 < col_count:
+                scores = pair_scores(unit, near + 1)
+            add_tile(unit, near, current, col_norm)
 
     pair = col + 1 - 2 * (col % 2)
     far = (col + 2) % col_count
@@ -264,13 +275,17 @@
             recv_sem=part_recv.at[at], device_id=(row, target), device_id_type=mesh_ids,
         )
 
-    last = (UNITS - 2, UNITS - 1)
-    for unit in last:
-        wait_unit(unit)
-    last_norms = [unit_norm(unit) for unit in last]
-    for at, near in enumerate((far_pair, pair, far, col)):
-        for unit, col_norm in zip(last, last_norms):
-            add_tile(unit, near, col_norm)
+    last = UNITS - 2
+    wait_unit(last)
+    wait_unit(last + 1)
+    order = (far_pair, pair, far, col)
+    scores = pair_scores(last, order[0])
+    last_norm = pair_norm(last)
+    for at, near in enumerate(order):
+        current = scores
+        if at + 1 < col_count:
+            scores = pair_scores(last, order[at + 1])
+        add_tile(last, near, current, last_norm)
         if at == 2:
             part_copy(0).wait_recv()
             acc[far] = acc[far] + parts[0]
@@ -313,16 +328,22 @@
     )
     gram = jnp.concatenate([packed[:, :eig_count], packed[:, eig_count:]], axis=0) / total_rows
 
-    down = lax.broadcasted_iota(jnp.int32, (eig_count, 1), 0)
+    down = lax.broadcasted_iota(jnp.int32, (8, 2 * eig_count), 0)
     at_row = lax.broadcasted_iota(jnp.int32, (eig_count, eig_count), 0)
     at_col = lax.broadcasted_iota(jnp.int32, (eig_count, eig_count), 1)
     diagonal = at_row == at_col
     work = jnp.concatenate([diagonal.astype(jnp.float32), gram], axis=1)
+    groups = [work[start : start + 8, :] for start in range(0, eig_count, 8)]
     for step in range(eig_count - 1):
-        at = eig_count + step
-        pivot = work[step : step + 1, :]
-        ratio = work[:, at : at + 1] * (1.0 / pivot[:, at : at + 1])
-        work = work - jnp.where(down > step, ratio, 0.0) * pivot
+        at, group, inner = eig_count + step, step // 8, step % 8
+        column = [
+            jnp.broadcast_to(held[:, at : at + 1], (8, 2 * eig_count)) for held in groups[group:]
+        ]
+        scaled = groups[group][inner : inner + 1, :] / column[0][inner : inner + 1, :]
+        column[0] = jnp.where(down > inner, column[0], 0.0)
+        for place, values in enumerate(column):
+            groups[group + place] = groups[group + place] - values * scaled
+    work = jnp.concatenate(groups, axis=0)
     pivots = jnp.sum(jnp.where(diagonal, work[:, eig_count:], 0.0), axis=1, keepdims=True)
     inverse = work[:, :eig_count] * lax.rsqrt(pivots)
     out_ref[...] = jnp.dot(

time: 77.2 us -> 77 us (level)
  no operation moved by 1% of the time
where the time goes in v4:
time: 77 us; the launch traced here: 76.9 us
  Pallas kernels  75.3 us (98%)
  local copies, waits for them, and re-layouts  1.57 us (2%)
    pallas_call x1, Pallas kernels, per_device_full(): pl.pallas_call(functools.partial(whole_kernel, total_rows), out_shape=jax...  75.3 us
    unnamed x1, local copies, waits for them, and re-layouts  1.57 us

profile of v4, /device:TPU:0, one launch (start us, length us, event | category | flops | bytes accessed | tf_op | source)
XLA Modules:
  0.0 76.9 jit_solution(278910152323985454)
XLA Ops:
  0.0 75.3 %shard_map.28 = f32[64,512]{1,0:T(8,128)} custom-call(bf16[2048,1024]{1,0:T(8,128)(2,1)} %x_hbm.1, bf16[64,512]{1,0:T(8,128)(2,1)} %v_hbm.1), custom_call_target="tpu_custom_call" | custom-call | tf_op jit(solution)/shard_map/pallas_call | solution.py:368
  75.3 1.6 %copy.4 = f32[64,512]{1,0:T(8,128)} copy(f32[64,512]{1,0:T(8,128)} %shard_map.28) | data formatting | bytes 262144

commit v5 on v4

--- a/solution.py
+++ b/solution.py
@@ -152,6 +152,7 @@
     col_count, padded, block_rows = acc.shape
     eig_count = own_v.shape[0]
     half = block_rows // 2
+    quarter = half // 2
     width = own_x.shape[1]
     mesh_ids = pl.DeviceIdType.MESH
 
@@ -170,10 +171,10 @@
     def unit_copies(source, target, bits):
         if source < 2:
             start = pl.multiple_of(col * block_rows + source * half, half)
-            x_src = x_hbm.at[pl.ds(start, half), :]
+            x_src = [x_hbm.at[pl.ds(start + at * quarter, quarter), :] for at in range(2)]
             v_src = v_hbm.at[:, pl.ds(source * half, half)]
         else:
-            x_src = far_x.at[source]
+            x_src = [far_x.at[source, pl.ds(at * quarter, quarter), :] for at in range(2)]
             v_src = far_v.at[source]
         partner = (across(row, bits), col)
         return (
@@ -181,10 +182,13 @@
                 src_ref=v_src, dst_ref=far_v.at[target], send_sem=v_send.at[target],
                 recv_sem=v_recv.at[target], device_id=partner, device_id_type=mesh_ids,
             ),
+        ) + tuple(
             pltpu.make_async_remote_copy(
-                src_ref=x_src, dst_ref=far_x.at[target], send_sem=x_send.at[target],
-                recv_sem=x_recv.at[target], device_id=partner, device_id_type=mesh_ids,
-            ),
+                src_ref=x_src[at], dst_ref=far_x.at[target, pl.ds(at * quarter, quarter), :],
+                send_sem=x_send.at[at, target], recv_sem=x_recv.at[at, target],
+                device_id=partner, device_id_type=mesh_ids,
+            )
+            for at in range(2)
         )
 
     def start_unit(item):
@@ -193,7 +197,9 @@
 
     def wait_unit(target):
         pltpu.make_async_copy(far_v.at[target], far_v.at[target], v_recv.at[target]).wait()
-        pltpu.make_async_copy(far_x.at[target], far_x.at[target], x_recv.at[target]).wait()
+        for at in range(2):
+            piece = far_x.at[target, pl.ds(at * quarter, quarter), :]
+            pltpu.make_async_copy(piece, piece, x_recv.at[at, target]).wait()
 
     for item in FIRST_SENDS:
         start_unit(item)
@@ -288,9 +294,11 @@
         add_tile(last, near, current, last_norm)
         if at == 2:
             part_copy(0).wait_recv()
+            part_copy(1).start()
             acc[far] = acc[far] + parts[0]
-        if at < 3:
-            part_copy(at).start()
+            part_copy(2).start()
+        if at == 0:
+            part_copy(0).start()
     part_copy(1).wait_recv()
     part_copy(2).wait_recv()
     total = acc[col] + parts[1] + parts[2]
@@ -368,7 +376,7 @@
     return pl.pallas_call(
         functools.partial(whole_kernel, total_rows),
         out_shape=jax.ShapeDtypeStruct((eig_count, block_rows), jnp.float32),
-        in_specs=[pl.BlockSpec(memory_space=pl.ANY)] * 2,
+        in_specs=[pl.BlockSpec(memory_space=pltpu.HBM)] * 2,
         out_specs=pl.BlockSpec(memory_space=pltpu.VMEM),
         scratch_shapes=[
             pltpu.VMEM((near_rows, width), jnp.bfloat16),
@@ -383,8 +391,8 @@
             pltpu.VMEM((col_count, eig_count // 2, 2 * eig_count), jnp.float32),
             dma(()),
             dma(()),
-            dma((UNITS,)),
-            dma((UNITS,)),
+            dma((2, UNITS)),
+            dma((2, UNITS)),
             dma((UNITS,)),
             dma((UNITS,)),
             dma((col_count - 1,)),
@@ -395,7 +403,7 @@
             dma((col_count - 1,)),
         ],
         compiler_params=pltpu.CompilerParams(
-            collective_id=0, has_side_effects=True, vmem_limit_bytes=60 * 1024 * 1024
+            collective_id=0, has_side_effects=True, vmem_limit_bytes=48 * 1024 * 1024
         ),
     )(embeddings, vectors)
 

time: 77 us -> 78.4 us (1.018)
  local copies, waits for them, and re-layouts: 1.57 us -> 3.68 us
  Pallas kernels: 75.3 us -> 74.5 us
    unnamed x1 -> x5, local copies, waits for them, and re-layouts: 1.57 us -> 3.68 us
where the time goes in v5:
time: 78.4 us; the launch traced here: 78.2 us
  Pallas kernels  74.5 us (95%)
  local copies, waits for them, and re-layouts  3.68 us (5%)
    pallas_call x1, Pallas kernels, per_device_full(): pl.pallas_call(functools.partial(whole_kernel, total_rows), out_shape=jax...  74.5 us
    unnamed x5, local copies, waits for them, and re-layouts  3.68 us

profile of v5, /device:TPU:0, one launch (start us, length us, event | category | flops | bytes accessed | tf_op | source)
XLA Modules:
  0.0 78.2 jit_solution(2607799657534990096)
XLA Ops:
  0.0 0.0 copy-start
  0.0 2.2 %copy-done = bf16[2048,1024]{1,0:T(8,128)(2,1)S(1)} copy-done((bf16[2048,1024]{1,0:T(8,128)(2,1)S(1)}, bf16[2048,1024]{1,0:T(8,128)(2,1)}, u32[]{:S(2)}) %copy-start) | copy-done | bytes 4194328
  2.2 0.0 copy-start.1
  2.2 0.8 %copy-done.1 = bf16[64,512]{1,0:T(8,128)(2,1)S(1)} copy-done((bf16[64,512]{1,0:T(8,128)(2,1)S(1)}, bf16[64,512]{1,0:T(8,128)(2,1)}, u32[]{:S(2)}) %copy-start.1) | copy-done | bytes 65560
  3.0 74.5 %shard_map.28 = f32[64,512]{1,0:T(8,128)S(1)} custom-call(bf16[2048,1024]{1,0:T(8,128)(2,1)S(1)} %copy-done, bf16[64,512]{1,0:T(8,128)(2,1)S(1)} %copy-done.1), custom_call_target="tpu_custom_call" | custom-call | tf_op jit(solution)/shard_map/pallas_call | solution.py:376
  77.6 0.7 copy.4
Async XLA Ops:
  0.0 2.2 %copy-start = (bf16[2048,1024]{1,0:T(8,128)(2,1)S(1)}, bf16[2048,1024]{1,0:T(8,128)(2,1)}, u32[]{:S(2)}) copy-start(bf16[2048,1024]{1,0:T(8,128)(2,1)} %x_hbm.1) | copy-start | bytes 12582916
  2.2 0.8 %copy-start.1 = (bf16[64,512]{1,0:T(8,128)(2,1)S(1)}, bf16[64,512]{1,0:T(8,128)(2,1)}, u32[]{:S(2)}) copy-start(bf16[64,512]{1,0:T(8,128)(2,1)} %v_hbm.1) | copy-start | bytes 196612

commit v6 on v5

--- a/solution.py
+++ b/solution.py
@@ -274,11 +274,16 @@
     far = (col + 2) % col_count
     far_pair = col_count - 1 - col
 
-    def part_copy(at):
+    split = eig_count // 2 + 8
+    pieces = (pl.ds(0, split), pl.ds(split, padded - split))
+
+    def part_copy(at, piece):
         source, target = ((far_pair, pair), (pair, pair), (far, far))[at]
+        rows = pieces[piece]
         return pltpu.make_async_remote_copy(
-            src_ref=acc.at[source], dst_ref=parts.at[at], send_sem=part_send.at[at],
-            recv_sem=part_recv.at[at], device_id=(row, target), device_id_type=mesh_ids,
+            src_ref=acc.at[source, rows, :], dst_ref=parts.at[at, rows, :],
+            send_sem=part_send.at[piece, at], recv_sem=part_recv.at[piece, at],
+            device_id=(row, target), device_id_type=mesh_ids,
         )
 
     last = UNITS - 2
@@ -292,15 +297,18 @@
         if at + 1 < col_count:
             scores = pair_scores(last, order[at + 1])
         add_tile(last, near, current, last_norm)
+        if at == 0:
+            part_copy(0, 0).start()
+            part_copy(0, 1).start()
         if at == 2:
-            part_copy(0).wait_recv()
-            part_copy(1).start()
-            acc[far] = acc[far] + parts[0]
-            part_copy(2).start()
-        if at == 0:
-            part_copy(0).start()
-    part_copy(1).wait_recv()
-    part_copy(2).wait_recv()
+            for piece, rows in enumerate(pieces):
+                part_copy(0, piece).wait_recv()
+                acc[far, rows, :] = acc[far, rows, :] + parts[0, rows, :]
+                part_copy(2, piece).start()
+                part_copy(1, piece).start()
+    for at in (1, 2):
+        for piece in range(2):
+            part_copy(at, piece).wait_recv()
     total = acc[col] + parts[1] + parts[2]
     degree = jnp.sum(total[eig_count:, :], axis=0, keepdims=True)
     smoothed = total[:eig_count, :] / degree
@@ -342,15 +350,26 @@
     diagonal = at_row == at_col
     work = jnp.concatenate([diagonal.astype(jnp.float32), gram], axis=1)
     groups = [work[start : start + 8, :] for start in range(0, eig_count, 8)]
-    for step in range(eig_count - 1):
+    def spread(held, at):
+        return jnp.broadcast_to(held[:, at : at + 1], (8, 2 * eig_count))
+
+    for step in range(0, eig_count, 2):
         at, group, inner = eig_count + step, step // 8, step % 8
-        column = [
-            jnp.broadcast_to(held[:, at : at + 1], (8, 2 * eig_count)) for held in groups[group:]
-        ]
-        scaled = groups[group][inner : inner + 1, :] / column[0][inner : inner + 1, :]
-        column[0] = jnp.where(down > inner, column[0], 0.0)
-        for place, values in enumerate(column):
-            groups[group + place] = groups[group + place] - values * scaled
+        first = [spread(held, at) for held in groups[group:]]
+        second = [spread(held, at + 1) for held in groups[group:]]
+        upper = groups[group][inner : inner + 1, :]
+        lower = groups[group][inner + 1 : inner + 2, :]
+        top = 1.0 / first[0][inner : inner + 1, :]
+        side = second[0][inner : inner + 1, :] * top
+        cross = first[0][inner + 1 : inner + 2, :]
+        lower = lower - cross * top * upper
+        bottom = 1.0 / (second[0][inner + 1 : inner + 2, :] - cross * side)
+        upper, lower = upper * top, lower * bottom
+        for place in range(len(first)):
+            one, two = first[place], second[place] - first[place] * side
+            if place == 0:
+                one, two = jnp.where(down > inner, one, 0.0), jnp.where(down > inner + 1, two, 0.0)
+            groups[group + place] = groups[group + place] - one * upper - two * lower
     work = jnp.concatenate(groups, axis=0)
     pivots = jnp.sum(jnp.where(diagonal, work[:, eig_count:], 0.0), axis=1, keepdims=True)
     inverse = work[:, :eig_count] * lax.rsqrt(pivots)
@@ -362,7 +381,8 @@
         for copy in unit_copies(*item):
             copy.wait_send()
     for at in range(3):
-        part_copy(at).wait_send()
+        for piece in range(2):
+            part_copy(at, piece).wait_send()
 
 
 def per_device_full(total_rows, row_count, embeddings, vectors, block_pairs):
@@ -376,7 +396,7 @@
     return pl.pallas_call(
         functools.partial(whole_kernel, total_rows),
         out_shape=jax.ShapeDtypeStruct((eig_count, block_rows), jnp.float32),
-        in_specs=[pl.BlockSpec(memory_space=pltpu.HBM)] * 2,
+        in_specs=[pl.BlockSpec(memory_space=pl.ANY)] * 2,
         out_specs=pl.BlockSpec(memory_space=pltpu.VMEM),
         scratch_shapes=[
             pltpu.VMEM((near_rows, width), jnp.bfloat16),
@@ -395,15 +415,15 @@
             dma((2, UNITS)),
             dma((UNITS,)),
             dma((UNITS,)),
-            dma((col_count - 1,)),
-            dma((col_count - 1,)),
+            dma((2, col_count - 1)),
+            dma((2, col_count - 1)),
             dma((row_count - 1,)),
             dma((row_count - 1,)),
             dma((col_count - 1,)),
             dma((col_count - 1,)),
         ],
         compiler_params=pltpu.CompilerParams(
-            collective_id=0, has_side_effects=True, vmem_limit_bytes=48 * 1024 * 1024
+            collective_id=0, has_side_effects=True, vmem_limit_bytes=60 * 1024 * 1024
         ),
     )(embeddings, vectors)
 

time: 78.4 us -> 73.4 us (0.936)
  Pallas kernels: 74.5 us -> 71.6 us
  local copies, waits for them, and re-layouts: 3.68 us -> 1.57 us
    pallas_call x1, Pallas kernels: 74.5 us -> 71.6 us  [per_device_full(): pl.pallas_call(functools.partial(whole_kernel, total_rows), out_shape=jax...]
    unnamed x5 -> x1, local copies, waits for them, and re-layouts: 3.68 us -> 1.57 us
where the time goes in v6:
time: 73.4 us; the launch traced here: 73.2 us
  Pallas kernels  71.6 us (98%)
  local copies, waits for them, and re-layouts  1.57 us (2%)
    pallas_call x1, Pallas kernels, per_device_full(): pl.pallas_call(functools.partial(whole_kernel, total_rows), out_shape=jax...  71.6 us
    unnamed x1, local copies, waits for them, and re-layouts  1.57 us

profile of v6, /device:TPU:0, one launch (start us, length us, event | category | flops | bytes accessed | tf_op | source)
XLA Modules:
  0.0 73.2 jit_solution(13870086366345556417)
XLA Ops:
  0.0 71.6 %shard_map.28 = f32[64,512]{1,0:T(8,128)} custom-call(bf16[2048,1024]{1,0:T(8,128)(2,1)} %x_hbm.1, bf16[64,512]{1,0:T(8,128)(2,1)} %v_hbm.1), custom_call_target="tpu_custom_call" | custom-call | tf_op jit(solution)/shard_map/pallas_call | solution.py:396
  71.7 1.6 %copy.4 = f32[64,512]{1,0:T(8,128)} copy(f32[64,512]{1,0:T(8,128)} %shard_map.28) | data formatting | bytes 262144

commit v7 on v6

--- a/solution.py
+++ b/solution.py
@@ -195,11 +195,29 @@
         for copy in unit_copies(*item):
             copy.start()
 
+    def wait_v(target):
+        pltpu.make_async_copy(far_v.at[target], far_v.at[target], v_recv.at[target]).wait()
+
+    def wait_x(target, at):
+        piece = far_x.at[target, pl.ds(at * quarter, quarter), :]
+        pltpu.make_async_copy(piece, piece, x_recv.at[at, target]).wait()
+
     def wait_unit(target):
-        pltpu.make_async_copy(far_v.at[target], far_v.at[target], v_recv.at[target]).wait()
+        wait_v(target)
         for at in range(2):
-            piece = far_x.at[target, pl.ds(at * quarter, quarter), :]
-            pltpu.make_async_copy(piece, piece, x_recv.at[at, target]).wait()
+            wait_x(target, at)
+
+    def relay(first):
+        copies = [unit_copies(*item) for item in RELAYS[first]]
+        wait_v(first)
+        wait_v(first + 1)
+        for held in copies:
+            held[0].start()
+        for at in range(2):
+            wait_x(first, at)
+            wait_x(first + 1, at)
+            for held in copies:
+                held[1 + at].start()
 
     for item in FIRST_SENDS:
         start_unit(item)
@@ -240,7 +258,7 @@
             cols_v, affinity.astype(jnp.bfloat16), preferred_element_type=jnp.float32
         )
 
-    @pl.loop(0, UNITS // 2 - 1)
+    @pl.loop(0, UNITS // 2 - 2)
     def _(pair_at):
         unit = pair_at * 2
 
@@ -248,13 +266,10 @@
         def _():
             acc[col] = jnp.zeros((padded, block_rows), jnp.float32)
 
-        for first, items in RELAYS.items():
+        for first in (4, 8):
             @pl.when(unit == first)
-            def _(first=first, items=items):
-                wait_unit(first)
-                wait_unit(first + 1)
-                for item in items:
-                    start_unit(item)
+            def _(first=first):
+                relay(first)
 
         for first in (2, 6, 10):
             @pl.when(unit == first)
@@ -287,25 +302,31 @@
         )
 
     last = UNITS - 2
+    relay(last - 2)
+    norms = {last - 2: pair_norm(last - 2)}
+
+    def add_last(unit, near):
+        add_tile(unit, near, pair_scores(unit, near), norms[unit])
+
+    add_last(last - 2, far_pair)
+    add_last(last - 2, pair)
     wait_unit(last)
     wait_unit(last + 1)
-    order = (far_pair, pair, far, col)
-    scores = pair_scores(last, order[0])
-    last_norm = pair_norm(last)
-    for at, near in enumerate(order):
-        current = scores
-        if at + 1 < col_count:
-            scores = pair_scores(last, order[at + 1])
-        add_tile(last, near, current, last_norm)
-        if at == 0:
-            part_copy(0, 0).start()
-            part_copy(0, 1).start()
-        if at == 2:
-            for piece, rows in enumerate(pieces):
-                part_copy(0, piece).wait_recv()
-                acc[far, rows, :] = acc[far, rows, :] + parts[0, rows, :]
-                part_copy(2, piece).start()
-                part_copy(1, piece).start()
+    norms[last] = pair_norm(last)
+    add_last(last, far_pair)
+    part_copy(0, 0).start()
+    part_copy(0, 1).start()
+    for near in (pair, far):
+        add_last(last, near)
+        if near is pair:
+            add_last(last - 2, far)
+    for piece, rows in enumerate(pieces):
+        part_copy(0, piece).wait_recv()
+        acc[far, rows, :] = acc[far, rows, :] + parts[0, rows, :]
+        part_copy(2, piece).start()
+        part_copy(1, piece).start()
+    add_last(last - 2, col)
+    add_last(last, col)
     for at in (1, 2):
         for piece in range(2):
             part_copy(at, piece).wait_recv()

time: 73.4 us -> 72.7 us (level)
  no operation moved by 1% of the time
where the time goes in v7:
time: 72.7 us; the launch traced here: 72.6 us
  Pallas kernels  71 us (98%)
  local copies, waits for them, and re-layouts  1.57 us (2%)
    pallas_call x1, Pallas kernels, per_device_full(): pl.pallas_call(functools.partial(whole_kernel, total_rows), out_shape=jax...  71 us
    unnamed x1, local copies, waits for them, and re-layouts  1.57 us

profile of v7, /device:TPU:0, one launch (start us, length us, event | category | flops | bytes accessed | tf_op | source)
XLA Modules:
  0.0 72.6 jit_solution(10839790430127554692)
XLA Ops:
  0.0 71.0 %shard_map.28 = f32[64,512]{1,0:T(8,128)} custom-call(bf16[2048,1024]{1,0:T(8,128)(2,1)} %x_hbm.1, bf16[64,512]{1,0:T(8,128)(2,1)} %v_hbm.1), custom_call_target="tpu_custom_call" | custom-call | tf_op jit(solution)/shard_map/pallas_call | solution.py:417
  71.0 1.6 %copy.4 = f32[64,512]{1,0:T(8,128)} copy(f32[64,512]{1,0:T(8,128)} %shard_map.28) | data formatting | bytes 262144

commit v8 on v7

--- a/solution.py
+++ b/solution.py
@@ -289,8 +289,8 @@
     far = (col + 2) % col_count
     far_pair = col_count - 1 - col
 
-    split = eig_count // 2 + 8
-    pieces = (pl.ds(0, split), pl.ds(split, padded - split))
+    third = padded // 3
+    pieces = tuple(pl.ds(start, third) for start in range(0, padded, third))
 
     def part_copy(at, piece):
         source, target = ((far_pair, pair), (pair, pair), (far, far))[at]
@@ -314,8 +314,8 @@
     wait_unit(last + 1)
     norms[last] = pair_norm(last)
     add_last(last, far_pair)
-    part_copy(0, 0).start()
-    part_copy(0, 1).start()
+    for piece in range(3):
+        part_copy(0, piece).start()
     for near in (pair, far):
         add_last(last, near)
         if near is pair:
@@ -328,7 +328,7 @@
     add_last(last - 2, col)
     add_last(last, col)
     for at in (1, 2):
-        for piece in range(2):
+        for piece in range(3):
             part_copy(at, piece).wait_recv()
     total = acc[col] + parts[1] + parts[2]
     degree = jnp.sum(total[eig_count:, :], axis=0, keepdims=True)
@@ -402,7 +402,7 @@
         for copy in unit_copies(*item):
             copy.wait_send()
     for at in range(3):
-        for piece in range(2):
+        for piece in range(3):
             part_copy(at, piece).wait_send()
 
 
@@ -436,8 +436,8 @@
             dma((2, UNITS)),
             dma((UNITS,)),
             dma((UNITS,)),
-            dma((2, col_count - 1)),
-            dma((2, col_count - 1)),
+            dma((3, col_count - 1)),
+            dma((3, col_count - 1)),
             dma((row_count - 1,)),
             dma((row_count - 1,)),
             dma((col_count - 1,)),

time: 72.7 us -> 72.3 us (level)
  no operation moved by 1% of the time
where the time goes in v8:
time: 72.3 us; the launch traced here: 72.2 us
  Pallas kernels  70.6 us (98%)
  local copies, waits for them, and re-layouts  1.57 us (2%)
    pallas_call x1, Pallas kernels, per_device_full(): pl.pallas_call(functools.partial(whole_kernel, total_rows), out_shape=jax...  70.6 us
    unnamed x1, local copies, waits for them, and re-layouts  1.57 us

profile of v8, /device:TPU:0, one launch (start us, length us, event | category | flops | bytes accessed | tf_op | source)
XLA Modules:
  0.0 72.2 jit_solution(114150952925582282)
XLA Ops:
  0.0 70.6 %shard_map.28 = f32[64,512]{1,0:T(8,128)} custom-call(bf16[2048,1024]{1,0:T(8,128)(2,1)} %x_hbm.1, bf16[64,512]{1,0:T(8,128)(2,1)} %v_hbm.1), custom_call_target="tpu_custom_call" | custom-call | tf_op jit(solution)/shard_map/pallas_call | solution.py:417
  70.6 1.6 %copy.4 = f32[64,512]{1,0:T(8,128)} copy(f32[64,512]{1,0:T(8,128)} %shard_map.28) | data formatting | bytes 262144
